TPU v7x, 32 devices: a whole 2x2x4 slice. The times are simulated.
32 devices in a mesh: req: 8 (over z, x), kv: 4 (over y, core).
Axes of the slice: x: 2, y: 2, z: 4, core: 2. Of those that a mesh axis runs over, the one named last changes fastest.
Arguments:
- residual_in: bfloat16 [16, 2560], P('req', 'kv'), may hold values from -8 to 8
- queries: bfloat16 [16, 2560], P('req', 'kv'), may hold values from -480 to 480
- fresh_token_keys: bfloat16 [16, 512], P('req', 'kv'), may hold values from -6 to 6
- fresh_token_values: bfloat16 [16, 512], P('req', 'kv'), may hold values from -6 to 6
- cached_key_slots: bfloat16 [16, 4096, 512], P('req', None, 'kv'), may hold values from -6 to 6
- cached_value_slots: bfloat16 [16, 4096, 512], P('req', None, 'kv'), may hold values from -6 to 6
- lengths: int32 [16], replicated, may hold values from 1 to 4096, as said below
- slot_order: int32 [16], replicated, may hold values from 0 to 15, as said below
- out_proj: bfloat16 [2560, 2560], P('kv'), may hold values from -0.5 to 0.5
- norm_gain: bfloat16 [2560], P('kv'), may hold values from 0.5 to 1.5
- expert_ids: int32 [16, 6], replicated, may hold values from 0 to 7, all different within a row; in each aligned block of 16 rows (0 to 15, 16 to 31, ...) at most 16 rows name the same one
- gate_values: float32 [16, 6], replicated, may hold values from 0.1 to 0.5
- gate_proj: bfloat16 [8, 2560, 1536], P('req', None, 'kv'), may hold values from -0.125 to 0.125
- up_proj: bfloat16 [8, 2560, 1536], P('req', None, 'kv'), may hold values from -0.125 to 0.125
- down_proj: bfloat16 [8, 1536, 2560], P('req', 'kv'), may hold values from -0.15625 to 0.15625
Outputs:
- layer_out: bfloat16 [16, 2560], P('req', 'kv')
Inputs may be any that keep to these rules, and one draw needn't show every extreme that they name: `lengths`: each request's count of cached positions; some request has exactly 4096. A permutation of the requests: slot s serves request slot_order[s], and cached_key_slots[s], cached_value_slots[s] hold that request's cache. Requests sorted by decreasing length are dealt to the 8 groups of 2 consecutive slots, one round forward, the next backward. `expert_ids`: each token names 6 different experts; no expert is named by more than 16 tokens, a bound that some block reaches.
All inputs are finite; a program needn't handle non-finite values.
Results may differ from a plain program's by a relative error of at most 0.012.
Values may be sent and summed in bfloat16 or wider, within the bound.
A program may use at most 64 MiB of HBM per device.

v0:
```python
import math

import jax
import jax.numpy as jnp
from jax import lax
from jax.sharding import PartitionSpec as P


def device_blocks(term, groups, parts):
    row_count = term.shape[0] // groups
    col_count = term.shape[1] // parts
    return (
        term.reshape(groups, row_count, parts, col_count)
        .transpose(0, 2, 1, 3)
        .reshape(groups * parts * row_count, col_count)
    )


def per_device(
    residual_in,
    queries,
    fresh_token_keys,
    fresh_token_values,
    cached_key_slots,
    cached_value_slots,
    lengths,
    slot_order,
    out_proj,
    norm_gain,
    expert_ids,
    gate_values,
    gate_proj,
    up_proj,
    down_proj,
):
    req_count = lax.axis_size("req")
    kv_count = lax.axis_size("kv")
    req_index = lax.axis_index("req")
    per_dev = residual_in.shape[0]
    head_dim = fresh_token_keys.shape[1]
    total_reqs = lengths.shape[0]
    model_width = out_proj.shape[1]
    all_queries, all_keys, all_values = (
        lax.all_gather(queries, "req", axis=0, tiled=True),
        lax.all_gather(fresh_token_keys, "req", axis=0, tiled=True),
        lax.all_gather(fresh_token_values, "req", axis=0, tiled=True),
    )
    served = lax.dynamic_slice_in_dim(slot_order, req_index * per_dev, per_dev)
    query_rows = all_queries[served].reshape(per_dev, -1, head_dim)
    self_key_row = all_keys[served]
    self_value_row = all_values[served]
    live_len = lengths[served]
    inv_root = 1.0 / math.sqrt(head_dim)
    scores = (
        jnp.einsum("rqd,rld->rql", query_rows, cached_key_slots, preferred_element_type=jnp.float32)
        * inv_root
    )
    positions = jnp.arange(cached_key_slots.shape[1])
    scores = jnp.where((positions[None, :] < live_len[:, None])[:, None, :], scores, -1e30)
    own_score = (
        jnp.einsum("rqd,rd->rq", query_rows, self_key_row, preferred_element_type=jnp.float32)
        * inv_root
    )
    highest = jnp.maximum(jnp.max(scores, axis=2), own_score)
    weights = jnp.exp(scores - highest[:, :, None])
    own_weight = jnp.exp(own_score - highest)
    totals = jnp.sum(weights, axis=2) + own_weight
    numerator = jnp.einsum(
        "rql,rld->rqd",
        weights.astype(jnp.bfloat16),
        cached_value_slots,
        preferred_element_type=jnp.float32,
    )
    own_low = lax.optimization_barrier(own_weight.astype(jnp.bfloat16)).astype(jnp.float32)
    numerator = numerator + own_low[:, :, None] * self_value_row.astype(jnp.float32)[:, None, :]
    attended = (numerator / totals[:, :, None]).astype(jnp.bfloat16).reshape(per_dev, -1)
    projected = jnp.dot(attended, out_proj, preferred_element_type=jnp.float32)
    placed = jnp.zeros((total_reqs, model_width), jnp.float32).at[served].set(projected)
    attn_part = lax.psum_scatter(
        device_blocks(placed, req_count, kv_count), ("req", "kv"), scatter_dimension=0, tiled=True
    )
    hidden = residual_in.astype(jnp.float32) + attn_part
    squares = lax.psum(jnp.sum(hidden * hidden, axis=1), "kv")
    normed = (
        hidden * lax.rsqrt(squares / model_width + 1e-06)[:, None] * norm_gain.astype(jnp.float32)
    ).astype(jnp.bfloat16)
    gathered = lax.all_gather(normed, ("req", "kv"), axis=0, tiled=True)
    tokens = (
        gathered.reshape(req_count, kv_count, per_dev, -1)
        .transpose(0, 2, 1, 3)
        .reshape(total_reqs, -1)
    )
    local_count = gate_proj.shape[0]
    capacity = min(2 * total_reqs * expert_ids.shape[1] // (local_count * req_count), total_reqs)
    expert = req_index * local_count + 0
    named_here = expert_ids == expert
    token_gate = jnp.sum(jnp.where(named_here, gate_values, 0.0), axis=1)
    uses_expert = jnp.any(named_here, axis=1)
    picked = jnp.nonzero(uses_expert, size=capacity, fill_value=0)[0].astype(jnp.int32)
    valid_rows = jnp.arange(capacity) < jnp.sum(uses_expert.astype(jnp.int32))
    row_block = tokens[picked]
    gate_h = jnp.dot(row_block, gate_proj[0], preferred_element_type=jnp.float32)
    up_h = jnp.dot(row_block, up_proj[0], preferred_element_type=jnp.float32)
    inner_act = (jax.nn.silu(gate_h) * up_h).astype(jnp.bfloat16)
    outputs = jnp.dot(inner_act, down_proj[0], preferred_element_type=jnp.float32)
    row_gate = jnp.where(valid_rows, token_gate[picked], 0.0)
    weighted_list = [outputs * row_gate[:, None]]
    picked_list = [picked]
    stacked_rows = jnp.concatenate(weighted_list, axis=0)
    stacked_idx = jnp.concatenate(picked_list, axis=0)
    mixture = jnp.zeros((total_reqs, model_width), jnp.float32).at[stacked_idx].add(stacked_rows)
    moe_part = lax.psum_scatter(
        device_blocks(mixture, req_count, kv_count), ("req", "kv"), scatter_dimension=0, tiled=True
    )
    return (hidden + moe_part).astype(jnp.bfloat16)


def solution(mesh):
    in_specs = (
        P("req", "kv"),
        P("req", "kv"),
        P("req", "kv"),
        P("req", "kv"),
        P("req", None, "kv"),
        P("req", None, "kv"),
        P(),
        P(),
        P("kv", None),
        P("kv"),
        P(),
        P(),
        P("req", None, "kv"),
        P("req", None, "kv"),
        P("req", "kv", None),
    )
    out_specs = P("req", "kv")
    return jax.shard_map(
        per_device, mesh=mesh, in_specs=in_specs, out_specs=out_specs, check_vma=False
    )
```

profile of v0, /device:TPU:0, one launch (start us, length us, event | category | flops | bytes accessed | tf_op | source)
XLA Modules:
  0.0 393.7 jit_solution(9540054352984748308)
XLA Ops:
  6.5 0.9 compare_select_fusion.2
  7.4 22.4 %all-gather.1 = bf16[8,2,128]{2,1,0:T(2,128)(2,1)S(1)} all-gather(bf16[1,2,128]{2,1,0:T(2,128)(2,1)} %bitcast.58), channel_id=1, replica_groups=mesh['req'=8,'kv'=4] {'req'}, dimensions={0}, use_global_device_ids=true | all-gather | bytes 4608 | tf_op jit(solution)/shard_map/all_gather | solution.py:45
  29.8 1.3 gather_fusion
  31.1 0.6 gather_fusion.2
  31.7 16.4 %all-gather.2 = bf16[8,2,128]{2,1,0:T(2,128)(2,1)S(1)} all-gather(bf16[1,2,128]{2,1,0:T(2,128)(2,1)} %bitcast.59), channel_id=1, replica_groups=mesh['req'=8,'kv'=4] {'req'}, dimensions={0}, use_global_device_ids=true | all-gather | bytes 4608 | tf_op jit(solution)/shard_map/all_gather | solution.py:46
  48.1 0.6 gather_fusion.3
  48.8 30.4 %all-gather = bf16[8,2,640]{2,1,0:T(2,128)(2,1)S(1)} all-gather(bf16[1,2,640]{2,1,0:T(2,128)(2,1)} %bitcast.57), channel_id=1, replica_groups=mesh['req'=8,'kv'=4] {'req'}, dimensions={0}, use_global_device_ids=true | all-gather | bytes 23040 | tf_op jit(solution)/shard_map/all_gather | solution.py:44
  79.1 0.6 gather_fusion.1
  79.9 2.4 fusion.47
  83.6 0.7 scatter_custom_fusion
  84.3 0.7 reshape.153
  85.0 1.0 copy.27
  86.0 0.8 reshape.154
  86.9 0.6 convert_reduce_fusion
  87.8 0.7 scatter_custom_fusion.1
  88.6 0.8 fusion.34
  89.3 0.7 gather_fusion.5
  90.0 0.7 compare_select_fusion.3
  90.7 116.7 %all-reduce.5.cloned.1.call-done = f32[64,640]{1,0:T(8,128)} async-done(((f32[64,640]{1,0:T(8,128)}), f32[64,640]{1,0:T(8,128)}) %all-reduce.5.cloned.1.call-update) | async-done | bytes 163856
  207.3 0.8 multiply_reduce_fusion
  208.2 7.1 %psum.7 = f32[2]{0:T(128)S(1)} all-reduce(f32[2]{0:T(128)S(1)} %multiply_reduce_fusion), channel_id=1, replica_groups=mesh['req'=8,'kv'=4] {'kv'}, use_global_device_ids=true, to_apply=%region_10.11 | all-reduce | flops 2 | bytes 16 | tf_op jit(solution)/shard_map/psum | solution.py:83
  215.3 0.8 fusion.39
  216.1 41.3 %all-gather.3 = bf16[32,2,640]{2,1,0:T(2,128)(2,1)S(1)} all-gather(bf16[1,2,640]{2,1,0:T(2,128)(2,1)S(1)} %fusion.39), channel_id=1, replica_groups=mesh['req'=8,'kv'=4] {'req','kv'}, dimensions={0}, use_global_device_ids=true | all-gather | bytes 84480 | tf_op jit(solution)/shard_map/all_gather | solution.py:87
  257.4 0.6 gather_fusion.4
  258.1 1.9 fusion.4
  260.0 3.7 convolution_multiply_fusion.1
  263.7 1.2 scatter_custom_fusion.2
  264.9 0.7 reshape.158
  265.7 1.0 copy.31
  266.7 0.8 reshape.159
  267.5 118.1 %all-reduce.7.cloned.1.call-done = f32[64,640]{1,0:T(8,128)} async-done(((f32[64,640]{1,0:T(8,128)}), f32[64,640]{1,0:T(8,128)}) %all-reduce.7.cloned.1.call-update) | async-done | bytes 163856
  385.6 1.3 fusion.35
  (42 shorter events, 2.0 us)
Async XLA Ops:
  6.5 76.5 %copy-start = (bf16[640,2560]{1,0:T(8,128)(2,1)S(1)}, bf16[640,2560]{1,0:T(8,128)(2,1)}, u32[]{:S(2)}) copy-start(bf16[640,2560]{1,0:T(8,128)(2,1)} %param.23) | copy-start | bytes 9830404
  6.5 200.8 %all-reduce.5.cloned.1.call-start = ((), (), s32[]{:S(2)}) async-start(), calls=%async_computation | async-start | bytes 327680
  79.7 2.8 copy-start.1
  83.0 3.8 copy-start.3
  83.0 3.8 copy-start.4
  83.0 124.3 %copy-start.2 = (bf16[2,640]{1,0:T(2,128)(2,1)S(1)}, bf16[2,640]{1,0:T(2,128)(2,1)}, u32[]{:S(2)}) copy-start(bf16[2,640]{1,0:T(2,128)(2,1)} %param.15) | copy-start | bytes 7684
  83.0 125.1 %copy-start.5 = (bf16[640]{0:T(1024)(128)(2,1)S(1)}, bf16[640]{0:T(1024)(128)(2,1)}, u32[]{:S(2)}) copy-start(bf16[640]{0:T(1024)(128)(2,1)} %param.24) | copy-start | bytes 3844
  86.8 298.8 %all-reduce.7.cloned.1.call-start = ((), (), s32[]{:S(2)}) async-start(), calls=%async_computation.1 | async-start | bytes 327680
Sparse Core Ops, SparseCore 0:
  86.9 120.3 all-reduce.4
  267.6 117.9 all-reduce.6
where the time goes:
time: 396 us; the launch traced here: 394 us
  waiting for transfers between devices  235 us (59%)
  blocking collectives  118 us (30%)
  between operations  13.6 us (3%)
  local copies, waits for them, and re-layouts  10.2 us (3%)
  matrix products  9.16 us (2%)
  other arithmetic  8.43 us (2%)
    unnamed x4, waiting for transfers between devices  235 us
    all_gather x1, blocking collectives, per_device(): gathered = lax.all_gather(normed, ('req', 'kv'), axis=0, tiled=True)  41.3 us
    all_gather x1, blocking collectives, per_device(): lax.all_gather(queries, 'req', axis=0, tiled=True)  30.4 us
    all_gather x1, blocking collectives, per_device(): lax.all_gather(fresh_token_keys, 'req', axis=0, tiled=True)  22.4 us
    all_gather x1, blocking collectives, per_device(): lax.all_gather(fresh_token_values, 'req', axis=0, tiled=True)  16.4 us
  transfers between devices with their start and end apart: 2, of which 2 were waited for; matrix products, arithmetic and copies ran while one was open for 1% of the time, Pallas kernels for 0%

commit v1 on v0

v1 whole, which is shorter than its diff:
```python
import functools
import math

import jax
import jax.numpy as jnp
from jax import lax
from jax.experimental import pallas as pl
from jax.experimental.pallas import tpu as pltpu
from jax.sharding import PartitionSpec as P

MESH = pl.DeviceIdType.MESH
F32 = jnp.float32
BF16 = jnp.bfloat16

PART_TYPE = F32
LAST_TYPE = F32


def layer_kernel(
    n_req,
    n_kv,
    len_ref,
    order_ref,
    ids_ref,
    gates_ref,
    gain_ref,
    res_hbm,
    q_hbm,
    k_hbm,
    v_hbm,
    keys_hbm,
    values_hbm,
    wo_hbm,
    wg_hbm,
    wu_hbm,
    wd_hbm,
    out_ref,
    rows,
    gains,
    keys,
    values,
    wo,
    wg,
    wu,
    wd,
    qmat,
    att,
    mine,
    part,
    normed,
    tokens,
    ysend,
    yrecv,
    zsend,
    zrecv,
    in_sem,
    w_sem,
    kv_send,
    kv_recv,
    req_send,
    req_recv,
):
    r = lax.axis_index("req")
    f = lax.axis_index("kv")
    per_dev, width = mine.shape
    q_width = q_hbm.shape[1]
    hd = k_hbm.shape[1]
    chunk = res_hbm.shape[1]
    heads = q_width // hd
    longest = keys.shape[1]
    total = n_req * per_dev

    places = (
        (q_hbm, 0, q_width),
        (k_hbm, q_width, hd),
        (v_hbm, q_width + hd, hd),
        (res_hbm, q_width + 2 * hd, chunk),
    )
    small = [
        pltpu.make_async_copy(src, rows.at[0, :, pl.ds(at, size)], in_sem.at[i])
        for i, (src, at, size) in enumerate(places)
    ]
    for c in small:
        c.start()
    loads = []
    for i in range(per_dev):
        loads.append(pltpu.make_async_copy(keys_hbm.at[i], keys.at[i], w_sem.at[2 * i]))
        loads.append(pltpu.make_async_copy(values_hbm.at[i], values.at[i], w_sem.at[2 * i + 1]))
    base = 2 * per_dev
    load_wo = pltpu.make_async_copy(wo_hbm, wo, w_sem.at[base])
    load_wg = pltpu.make_async_copy(wg_hbm.at[0], wg, w_sem.at[base + 1])
    load_wu = pltpu.make_async_copy(wu_hbm.at[0], wu, w_sem.at[base + 2])
    load_wd = pltpu.make_async_copy(wd_hbm.at[0], wd, w_sem.at[base + 3])
    for c in (*loads, load_wo, load_wg, load_wu, load_wd):
        c.start()

    def req_peer(d):
        return lax.rem(r + d, n_req)

    def kv_peer(k):
        return lax.rem(f + k, n_kv)

    barrier = pltpu.get_barrier_semaphore()
    for d in range(1, n_req):
        pl.semaphore_signal(barrier, inc=1, device_id=(req_peer(d), f), device_id_type=MESH)
    for k in range(1, n_kv):
        pl.semaphore_signal(barrier, inc=1, device_id=(r, kv_peer(k)), device_id_type=MESH)

    own_columns = pl.ds(pl.multiple_of(f * chunk, chunk), chunk)
    gains[:, own_columns] = gain_ref[...].astype(F32)
    qmat[...] = jnp.zeros_like(qmat)
    att[...] = jnp.zeros_like(att)

    for c in small:
        c.wait()
    pl.semaphore_wait(barrier, n_req + n_kv - 2)

    def to_req(stage, d, src, dst):
        return pltpu.make_async_remote_copy(
            src_ref=src,
            dst_ref=dst,
            send_sem=req_send.at[stage, d],
            recv_sem=req_recv.at[stage, d],
            device_id=(req_peer(d), f),
            device_id_type=MESH,
        )

    def to_kv(stage, k, src, dst):
        return pltpu.make_async_remote_copy(
            src_ref=src,
            dst_ref=dst,
            send_sem=kv_send.at[stage, k],
            recv_sem=kv_recv.at[stage, k],
            device_id=(r, kv_peer(k)),
            device_id_type=MESH,
        )

    first = [to_req(0, d, rows.at[0], rows.at[d]) for d in range(1, n_req)]
    for c in first:
        c.start()
    own_gain = gains.at[:, own_columns]
    gain_out = [to_kv(0, k, own_gain, own_gain) for k in range(1, n_kv)]
    for c in gain_out:
        c.start()
    for c in first:
        c.wait_recv()

    inv_root = 1.0 / math.sqrt(hd)
    served = [order_ref[r * per_dev + i] for i in range(per_dev)]
    positions = lax.broadcasted_iota(jnp.int32, (1, longest), 1)
    residual = []
    for i in range(per_dev):
        t = served[i]
        src = t // per_dev
        pair = rows[lax.rem(r - src + n_req, n_req)].astype(F32)
        which = lax.broadcasted_iota(jnp.int32, pair.shape, 0) == t - src * per_dev
        row = jnp.sum(jnp.where(which, pair, 0.0), axis=0, keepdims=True)
        residual.append(row[:, q_width + 2 * hd :])
        k_row = row[:, q_width : q_width + hd]
        v_row = row[:, q_width + hd : q_width + 2 * hd]
        for h in range(heads):
            qmat[i, h : h + 1, :] = row[:, h * hd : (h + 1) * hd]
        q = qmat[i]
        loads[2 * i].wait()
        scores = (
            lax.dot_general(
                q.astype(BF16), keys[i], (((1,), (1,)), ((), ())), preferred_element_type=F32
            )
            * inv_root
        )
        scores = jnp.where(positions < len_ref[t], scores, -1e30)
        own = jnp.sum(q * k_row, axis=1, keepdims=True) * inv_root
        highest = jnp.maximum(jnp.max(scores, axis=1, keepdims=True), own)
        weights = jnp.exp(scores - highest)
        own_weight = jnp.exp(own - highest)
        totals = jnp.sum(weights, axis=1, keepdims=True) + own_weight
        loads[2 * i + 1].wait()
        numerator = jnp.dot(weights.astype(BF16), values[i], preferred_element_type=F32)
        numerator = numerator + own_weight.astype(BF16).astype(F32) * v_row
        attended = numerator / totals
        for h in range(heads):
            att[i : i + 1, h * hd : (h + 1) * hd] = attended[h : h + 1, :]

    load_wo.wait()
    projected = jnp.dot(att[...].astype(BF16), wo[...], preferred_element_type=F32)
    mine[...] = projected[:per_dev]
    mine[:, own_columns] += jnp.concatenate(residual, axis=0)
    part[0] = mine[...].astype(part.dtype)
    second = [to_kv(1, k, part.at[0], part.at[k]) for k in range(1, n_kv)]
    for c in second:
        c.start()
    for c in gain_out:
        c.wait_recv()
    for c in second:
        c.wait_recv()
    hidden = mine[...]
    for k in range(1, n_kv):
        hidden = hidden + part[k].astype(F32)
    mine[...] = hidden
    squares = jnp.sum(hidden * hidden, axis=1, keepdims=True)
    normed[0] = (hidden * lax.rsqrt(squares / width + 1e-06) * gains[...]).astype(BF16)

    third = [to_req(1, d, normed.at[0], normed.at[d]) for d in range(1, n_req)]
    for c in third:
        c.start()

    gate_row = jnp.sum(jnp.where(ids_ref[...] == r, gates_ref[...], 0.0), axis=0, keepdims=True)
    token_of = lax.broadcasted_iota(jnp.int32, (total, total), 0)
    other_of = lax.broadcasted_iota(jnp.int32, (total, total), 1)
    gate = jnp.sum(jnp.where(token_of == other_of, gate_row, 0.0), axis=1, keepdims=True)
    slot_row = jnp.zeros((1, total), jnp.int32)
    slot_at = lax.broadcasted_iota(jnp.int32, (1, total), 1)
    for d in range(n_req):
        src = lax.rem(r - d + n_req, n_req)
        for i in range(per_dev):
            slot_row = jnp.where(
                slot_at == d * per_dev + i, order_ref[src * per_dev + i], slot_row
            )
    to_token = jnp.where(token_of == slot_row, 1.0, 0.0).astype(BF16)
    hidden_part = mine[:, own_columns]
    token_at = lax.broadcasted_iota(jnp.int32, (total, 1), 0)
    placed = jnp.zeros((total, chunk), F32)
    for i in range(per_dev):
        placed = placed + jnp.where(token_at == served[i], hidden_part[i : i + 1, :], 0.0)
    tokens[0:per_dev, :] = normed[0].astype(F32)
    load_wg.wait()
    load_wu.wait()
    load_wd.wait()

    for d, c in enumerate(third, 1):
        c.wait_recv()
        tokens[d * per_dev : (d + 1) * per_dev, :] = normed[d].astype(F32)
    x = tokens[...].astype(BF16)
    gate_h = jnp.dot(x, wg[...], preferred_element_type=F32)
    up_h = jnp.dot(x, wu[...], preferred_element_type=F32)
    inner = (gate_h / (1.0 + jnp.exp(-gate_h)) * up_h).astype(BF16)
    inner = jnp.dot(to_token, inner, preferred_element_type=F32).astype(BF16)

    fourth = []
    for k in range(1, n_kv):
        columns = pl.ds(pl.multiple_of(kv_peer(k) * chunk, chunk), chunk)
        y = jnp.dot(inner, wd[:, columns], preferred_element_type=F32) * gate
        ysend[k - 1] = y.astype(BF16)
        c = to_kv(2, k, ysend.at[k - 1], yrecv.at[k - 1])
        c.start()
        fourth.append(c)
    y = jnp.dot(inner, wd[:, own_columns], preferred_element_type=F32) * gate + placed
    for k, c in enumerate(fourth):
        c.wait_recv()
        y = y + yrecv[k].astype(F32)
    for p in range(n_req):
        zsend[p] = y[p * per_dev : (p + 1) * per_dev, :].astype(zsend.dtype)
    fifth = [to_req(2, d, zsend.at[req_peer(d)], zrecv.at[d - 1]) for d in range(1, n_req)]
    for c in fifth:
        c.start()
    z = zsend[r].astype(F32)
    for d, c in enumerate(fifth):
        c.wait_recv()
        z = z + zrecv[d].astype(F32)
    out_ref[...] = z.astype(out_ref.dtype)
    for c in (*first, *gain_out, *second, *third, *fourth, *fifth):
        c.wait_send()


def per_device(
    residual_in,
    queries,
    fresh_token_keys,
    fresh_token_values,
    cached_key_slots,
    cached_value_slots,
    lengths,
    slot_order,
    out_proj,
    norm_gain,
    expert_ids,
    gate_values,
    gate_proj,
    up_proj,
    down_proj,
):
    n_req = lax.axis_size("req")
    n_kv = lax.axis_size("kv")
    per_dev, chunk = residual_in.shape
    q_width = queries.shape[1]
    hd = fresh_token_keys.shape[1]
    width = out_proj.shape[1]
    total = lengths.shape[0]
    row_width = q_width + 2 * hd + chunk
    heads_up = -(-(q_width // hd) // 8) * 8
    vmem = pl.BlockSpec(memory_space=pltpu.VMEM)
    smem = pl.BlockSpec(memory_space=pltpu.SMEM)
    hbm = pl.BlockSpec(memory_space=pl.ANY)
    return pl.pallas_call(
        functools.partial(layer_kernel, n_req, n_kv),
        out_shape=jax.ShapeDtypeStruct((per_dev, chunk), BF16),
        in_specs=[smem, smem, vmem, vmem, vmem] + [hbm] * 10,
        out_specs=vmem,
        scratch_shapes=[
            pltpu.VMEM((n_req, per_dev, row_width), BF16),
            pltpu.VMEM((1, width), F32),
            pltpu.VMEM(cached_key_slots.shape, BF16),
            pltpu.VMEM(cached_value_slots.shape, BF16),
            pltpu.VMEM(out_proj.shape, BF16),
            pltpu.VMEM(gate_proj.shape[1:], BF16),
            pltpu.VMEM(up_proj.shape[1:], BF16),
            pltpu.VMEM(down_proj.shape[1:], BF16),
            pltpu.VMEM((per_dev, heads_up, hd), F32),
            pltpu.VMEM((8, q_width), F32),
            pltpu.VMEM((per_dev, width), F32),
            pltpu.VMEM((n_kv, per_dev, width), PART_TYPE),
            pltpu.VMEM((n_req, per_dev, width), BF16),
            pltpu.VMEM((total, width), F32),
            pltpu.VMEM((n_kv - 1, total, chunk), BF16),
            pltpu.VMEM((n_kv - 1, total, chunk), BF16),
            pltpu.VMEM((n_req, per_dev, chunk), LAST_TYPE),
            pltpu.VMEM((n_req - 1, per_dev, chunk), LAST_TYPE),
            pltpu.SemaphoreType.DMA((4,)),
            pltpu.SemaphoreType.DMA((2 * per_dev + 4,)),
            pltpu.SemaphoreType.DMA((3, n_kv)),
            pltpu.SemaphoreType.DMA((3, n_kv)),
            pltpu.SemaphoreType.DMA((3, n_req)),
            pltpu.SemaphoreType.DMA((3, n_req)),
        ],
        compiler_params=pltpu.CompilerParams(
            collective_id=0, has_side_effects=True, vmem_limit_bytes=56 * 1024 * 1024
        ),
        cost_estimate=pl.CostEstimate(
            flops=400_000_000, bytes_accessed=14_000_000, transcendentals=100_000
        ),
    )(
        lengths,
        slot_order,
        expert_ids.T,
        gate_values.T,
        norm_gain.reshape(1, -1),
        residual_in,
        queries,
        fresh_token_keys,
        fresh_token_values,
        cached_key_slots,
        cached_value_slots,
        out_proj,
        gate_proj,
        up_proj,
        down_proj,
    )


def solution(mesh):
    in_specs = (
        P("req", "kv"),
        P("req", "kv"),
        P("req", "kv"),
        P("req", "kv"),
        P("req", None, "kv"),
        P("req", None, "kv"),
        P(),
        P(),
        P("kv", None),
        P("kv"),
        P(),
        P(),
        P("req", None, "kv"),
        P("req", None, "kv"),
        P("req", "kv", None),
    )
    return jax.shard_map(
        per_device, mesh=mesh, in_specs=in_specs, out_specs=P("req", "kv"), check_vma=False
    )
```

time: 396 us -> 34.2 us (0.09)
  waiting for transfers between devices: 235 us -> 0 us
  blocking collectives: 118 us -> 0 us
  Pallas kernels: 0 us -> 31.5 us
  between operations: 13.6 us -> 0.01 us
  matrix products: 9.16 us -> 0 us
  other arithmetic: 8.43 us -> 0 us
  local copies, waits for them, and re-layouts: 10.2 us -> 2.53 us
    unnamed x4 -> x0, waiting for transfers between devices: 235 us -> none
    all_gather x4 -> x0, blocking collectives: 110 us -> none  [the longest x1 41.3 us: per_device(): gathered = lax.all_gather(normed, ('req', 'kv'), axis=0, tiled=True)]
    pallas_call x0 -> x1, Pallas kernels: none -> 31.5 us  [per_device(): pl.pallas_call(functools.partial(layer_kernel, n_req, n_kv), out_shape=ja...]
    dot_general x6 -> x0, matrix products: 9.16 us -> none  [the longest x1 3.72 us: per_device(): jnp.dot(inner_act, down_proj[0], preferred_element_type=jnp.float32)]
    psum x1 -> x0, blocking collectives: 7.14 us -> none  [per_device(): squares = lax.psum(jnp.sum(hidden * hidden, axis=1), 'kv')]
    gather x6 -> x0, local copies, waits for them, and re-layouts: 4.24 us -> none  [the longest x1 1.29 us: per_device(): live_len = lengths[served]]
  transfers between devices with their start and end apart: 2 -> 0, of which waited for: 2 -> 0; matrix products, arithmetic and copies ran while one was open for 1% -> 0% of each run, Pallas kernels for 0% -> 0%
where the time goes in v1:
time: 34.2 us; the launch traced here: 34 us
  Pallas kernels  31.5 us (92%)
  local copies, waits for them, and re-layouts  2.53 us (7%)
    pallas_call x1, Pallas kernels, per_device(): pl.pallas_call(functools.partial(layer_kernel, n_req, n_kv), out_shape=ja...  31.5 us
    unnamed x1, local copies, waits for them, and re-layouts  1.26 us
    reshape x1, local copies, waits for them, and re-layouts, per_device(): norm_gain.reshape(1, -1)  1.26 us

profile of v1, /device:TPU:0, one launch (start us, length us, event | category | flops | bytes accessed | tf_op | source)
XLA Modules:
  0.0 34.0 jit_solution(7809377842584830286)
XLA Ops:
  0.0 1.3 %reshape.3.gain_ref = bf16[1,640]{1,0:T(2,128)(2,1)} reshape(bf16[640]{0:T(1024)(128)(2,1)} %param.24) | data formatting | bytes 2560 | tf_op jit(solution)/shard_map/reshape | solution.py:336
  1.3 31.5 %shard_map.145 = bf16[2,640]{1,0:T(2,128)(2,1)} custom-call(s32[16]{0:T(128)} %len_ref.1, s32[16]{0:T(128)} %order_ref.1, s32[6,16]{1,0:T(8,128)} %bitcast.2, f32[6,16]{1,0:T(8,128)} %bitcast.3, bf16[1,640]{1,0:T(2,128)(2,1)} %reshape.3.gain_ref, bf16[2,640]{1,0:T(2,128)(2,1)} %res_hbm.1, bf16[2,640]{1,0:T(2,128)(2,1)} %q_hbm.1, bf16[2,128]{1,0:T(2,128)(2,1)} %k_hbm.1, ...), custom_call_target="tpu_custom_call" | custom-call | flops 400000000 | bytes 14000000 | tf_op jit(solution)/shard_map/pallas_call | solution.py:294
  32.8 1.3 %copy.17 = bf16[2,640]{1,0:T(2,128)(2,1)} copy(bf16[2,640]{1,0:T(2,128)(2,1)} %shard_map.145) | data formatting | bytes 5120

commit v2 on v1

--- a/solution.py
+++ b/solution.py
@@ -12,18 +12,18 @@
 F32 = jnp.float32
 BF16 = jnp.bfloat16
 
-PART_TYPE = F32
-LAST_TYPE = F32
+PART_TYPE = BF16
+LAST_TYPE = BF16
 
 
 def layer_kernel(
     n_req,
     n_kv,
-    len_ref,
-    order_ref,
-    ids_ref,
-    gates_ref,
-    gain_ref,
+    len_hbm,
+    order_hbm,
+    ids_hbm,
+    gates_hbm,
+    gain_hbm,
     res_hbm,
     q_hbm,
     k_hbm,
@@ -49,8 +49,6 @@
     part,
     normed,
     tokens,
-    ysend,
-    yrecv,
     zsend,
     zrecv,
     in_sem,
@@ -59,6 +57,13 @@
     kv_recv,
     req_send,
     req_recv,
+    z_sems,
+    len_ref,
+    order_ref,
+    ids_ref,
+    gates_ref,
+    gain_ref,
+    aux_sem,
 ):
     r = lax.axis_index("req")
     f = lax.axis_index("kv")
@@ -69,6 +74,20 @@
     heads = q_width // hd
     longest = keys.shape[1]
     total = n_req * per_dev
+
+    def req_peer(d):
+        return lax.rem(r + d, n_req)
+
+    def kv_peer(k):
+        return lax.rem(f + k, n_kv)
+
+    barrier = pltpu.get_barrier_semaphore()
+    for d in range(n_req - 1, -1, -1):
+        for k in range(n_kv):
+            if d or k:
+                pl.semaphore_signal(
+                    barrier, inc=1, device_id=(req_peer(d), kv_peer(k)), device_id_type=MESH
+                )
 
     places = (
         (q_hbm, 0, q_width),
@@ -82,6 +101,21 @@
     ]
     for c in small:
         c.start()
+    gain_in = pltpu.make_async_copy(gain_hbm, gain_ref, aux_sem.at[0])
+    aux = [
+        pltpu.make_async_copy(src, dst, aux_sem.at[i])
+        for i, (src, dst) in enumerate(
+            (
+                (len_hbm, len_ref),
+                (order_hbm, order_ref),
+                (ids_hbm, ids_ref),
+                (gates_hbm, gates_ref),
+            ),
+            1,
+        )
+    ]
+    for c in (gain_in, *aux):
+        c.start()
     loads = []
     for i in range(per_dev):
         loads.append(pltpu.make_async_copy(keys_hbm.at[i], keys.at[i], w_sem.at[2 * i]))
@@ -91,29 +125,18 @@
     load_wg = pltpu.make_async_copy(wg_hbm.at[0], wg, w_sem.at[base + 1])
     load_wu = pltpu.make_async_copy(wu_hbm.at[0], wu, w_sem.at[base + 2])
     load_wd = pltpu.make_async_copy(wd_hbm.at[0], wd, w_sem.at[base + 3])
-    for c in (*loads, load_wo, load_wg, load_wu, load_wd):
-        c.start()
-
-    def req_peer(d):
-        return lax.rem(r + d, n_req)
-
-    def kv_peer(k):
-        return lax.rem(f + k, n_kv)
-
-    barrier = pltpu.get_barrier_semaphore()
-    for d in range(1, n_req):
-        pl.semaphore_signal(barrier, inc=1, device_id=(req_peer(d), f), device_id_type=MESH)
-    for k in range(1, n_kv):
-        pl.semaphore_signal(barrier, inc=1, device_id=(r, kv_peer(k)), device_id_type=MESH)
+    for c in loads:
+        c.start()
 
     own_columns = pl.ds(pl.multiple_of(f * chunk, chunk), chunk)
-    gains[:, own_columns] = gain_ref[...].astype(F32)
+    gain_in.wait()
+    gains[:, own_columns] = gain_ref[...].astype(F32).reshape(1, -1)
     qmat[...] = jnp.zeros_like(qmat)
     att[...] = jnp.zeros_like(att)
 
     for c in small:
         c.wait()
-    pl.semaphore_wait(barrier, n_req + n_kv - 2)
+    pl.semaphore_wait(barrier, n_req * n_kv - 1)
 
     def to_req(stage, d, src, dst):
         return pltpu.make_async_remote_copy(
@@ -139,9 +162,13 @@
     for c in first:
         c.start()
     own_gain = gains.at[:, own_columns]
+    for c in (load_wo, load_wg, load_wu, load_wd):
+        c.start()
     gain_out = [to_kv(0, k, own_gain, own_gain) for k in range(1, n_kv)]
     for c in gain_out:
         c.start()
+    for c in (*aux, *loads, load_wo):
+        c.wait()
     for c in first:
         c.wait_recv()
 
@@ -161,7 +188,6 @@
         for h in range(heads):
             qmat[i, h : h + 1, :] = row[:, h * hd : (h + 1) * hd]
         q = qmat[i]
-        loads[2 * i].wait()
         scores = (
             lax.dot_general(
                 q.astype(BF16), keys[i], (((1,), (1,)), ((), ())), preferred_element_type=F32
@@ -174,14 +200,12 @@
         weights = jnp.exp(scores - highest)
         own_weight = jnp.exp(own - highest)
         totals = jnp.sum(weights, axis=1, keepdims=True) + own_weight
-        loads[2 * i + 1].wait()
         numerator = jnp.dot(weights.astype(BF16), values[i], preferred_element_type=F32)
         numerator = numerator + own_weight.astype(BF16).astype(F32) * v_row
         attended = numerator / totals
         for h in range(heads):
             att[i : i + 1, h * hd : (h + 1) * hd] = attended[h : h + 1, :]
 
-    load_wo.wait()
     projected = jnp.dot(att[...].astype(BF16), wo[...], preferred_element_type=F32)
     mine[...] = projected[:per_dev]
     mine[:, own_columns] += jnp.concatenate(residual, axis=0)
@@ -237,28 +261,35 @@
     inner = jnp.dot(to_token, inner, preferred_element_type=F32).astype(BF16)
 
     fourth = []
-    for k in range(1, n_kv):
+    for k in (*range(1, n_kv), 0):
         columns = pl.ds(pl.multiple_of(kv_peer(k) * chunk, chunk), chunk)
         y = jnp.dot(inner, wd[:, columns], preferred_element_type=F32) * gate
-        ysend[k - 1] = y.astype(BF16)
-        c = to_kv(2, k, ysend.at[k - 1], yrecv.at[k - 1])
-        c.start()
-        fourth.append(c)
-    y = jnp.dot(inner, wd[:, own_columns], preferred_element_type=F32) * gate + placed
-    for k, c in enumerate(fourth):
+        if k == 0:
+            y = y + placed
+        y = y.astype(zsend.dtype)
+        for p in range(n_req):
+            zsend[k, p] = y[p * per_dev : (p + 1) * per_dev, :]
+        for d in range(n_req):
+            if k == 0 and d == 0:
+                continue
+            c = pltpu.make_async_remote_copy(
+                src_ref=zsend.at[k, req_peer(d)],
+                dst_ref=zrecv.at[k, d],
+                send_sem=z_sems.at[0, k * n_req + d],
+                recv_sem=z_sems.at[1, k * n_req + d],
+                device_id=(req_peer(d), kv_peer(k)),
+                device_id_type=MESH,
+            )
+            c.start()
+            fourth.append((k, d, c))
+    z = zsend[0, r].astype(F32)
+    for k, d, c in fourth:
         c.wait_recv()
-        y = y + yrecv[k].astype(F32)
-    for p in range(n_req):
-        zsend[p] = y[p * per_dev : (p + 1) * per_dev, :].astype(zsend.dtype)
-    fifth = [to_req(2, d, zsend.at[req_peer(d)], zrecv.at[d - 1]) for d in range(1, n_req)]
-    for c in fifth:
-        c.start()
-    z = zsend[r].astype(F32)
-    for d, c in enumerate(fifth):
-        c.wait_recv()
-        z = z + zrecv[d].astype(F32)
+        z = z + zrecv[k, d].astype(F32)
     out_ref[...] = z.astype(out_ref.dtype)
-    for c in (*first, *gain_out, *second, *third, *fourth, *fifth):
+    for c in (*first, *gain_out, *second, *third):
+        c.wait_send()
+    for _, _, c in fourth:
         c.wait_send()
 
 
@@ -289,12 +320,11 @@
     row_width = q_width + 2 * hd + chunk
     heads_up = -(-(q_width // hd) // 8) * 8
     vmem = pl.BlockSpec(memory_space=pltpu.VMEM)
-    smem = pl.BlockSpec(memory_space=pltpu.SMEM)
     hbm = pl.BlockSpec(memory_space=pl.ANY)
     return pl.pallas_call(
         functools.partial(layer_kernel, n_req, n_kv),
         out_shape=jax.ShapeDtypeStruct((per_dev, chunk), BF16),
-        in_specs=[smem, smem, vmem, vmem, vmem] + [hbm] * 10,
+        in_specs=[hbm] * 15,
         out_specs=vmem,
         scratch_shapes=[
             pltpu.VMEM((n_req, per_dev, row_width), BF16),
@@ -311,16 +341,21 @@
             pltpu.VMEM((n_kv, per_dev, width), PART_TYPE),
             pltpu.VMEM((n_req, per_dev, width), BF16),
             pltpu.VMEM((total, width), F32),
-            pltpu.VMEM((n_kv - 1, total, chunk), BF16),
-            pltpu.VMEM((n_kv - 1, total, chunk), BF16),
-            pltpu.VMEM((n_req, per_dev, chunk), LAST_TYPE),
-            pltpu.VMEM((n_req - 1, per_dev, chunk), LAST_TYPE),
+            pltpu.VMEM((n_kv, n_req, per_dev, chunk), LAST_TYPE),
+            pltpu.VMEM((n_kv, n_req, per_dev, chunk), LAST_TYPE),
             pltpu.SemaphoreType.DMA((4,)),
             pltpu.SemaphoreType.DMA((2 * per_dev + 4,)),
-            pltpu.SemaphoreType.DMA((3, n_kv)),
-            pltpu.SemaphoreType.DMA((3, n_kv)),
-            pltpu.SemaphoreType.DMA((3, n_req)),
-            pltpu.SemaphoreType.DMA((3, n_req)),
+            pltpu.SemaphoreType.DMA((2, n_kv)),
+            pltpu.SemaphoreType.DMA((2, n_kv)),
+            pltpu.SemaphoreType.DMA((2, n_req)),
+            pltpu.SemaphoreType.DMA((2, n_req)),
+            pltpu.SemaphoreType.DMA((2, n_kv * n_req)),
+            pltpu.SMEM(lengths.shape, jnp.int32),
+            pltpu.SMEM(slot_order.shape, jnp.int32),
+            pltpu.VMEM(expert_ids.shape[::-1], jnp.int32),
+            pltpu.VMEM(gate_values.shape[::-1], F32),
+            pltpu.VMEM(norm_gain.shape, BF16),
+            pltpu.SemaphoreType.DMA((5,)),
         ],
         compiler_params=pltpu.CompilerParams(
             collective_id=0, has_side_effects=True, vmem_limit_bytes=56 * 1024 * 1024
@@ -333,7 +368,7 @@
         slot_order,
         expert_ids.T,
         gate_values.T,
-        norm_gain.reshape(1, -1),
+        norm_gain,
         residual_in,
         queries,
         fresh_token_keys,

time: 34.2 us -> 28.4 us (0.83)
  Pallas kernels: 31.5 us -> 26.9 us
  local copies, waits for them, and re-layouts: 2.53 us -> 1.26 us
    pallas_call x1, Pallas kernels: 31.5 us -> 26.9 us  [per_device(): pl.pallas_call(functools.partial(layer_kernel, n_req, n_kv), out_shape=ja...]
    reshape x1 -> x0, local copies, waits for them, and re-layouts: 1.26 us -> none  [per_device(): norm_gain.reshape(1, -1)]
where the time goes in v2:
time: 28.4 us; the launch traced here: 28.2 us
  Pallas kernels  26.9 us (95%)
  local copies, waits for them, and re-layouts  1.26 us (4%)
    pallas_call x1, Pallas kernels, per_device(): pl.pallas_call(functools.partial(layer_kernel, n_req, n_kv), out_shape=ja...  26.9 us
    unnamed x1, local copies, waits for them, and re-layouts  1.26 us

profile of v2, /device:TPU:0, one launch (start us, length us, event | category | flops | bytes accessed | tf_op | source)
XLA Modules:
  0.0 28.2 jit_solution(7365535569000525732)
XLA Ops:
  0.0 26.9 %shard_map.145 = bf16[2,640]{1,0:T(2,128)(2,1)} custom-call(s32[16]{0:T(128)} %len_hbm.1, s32[16]{0:T(128)} %order_hbm.1, s32[6,16]{1,0:T(8,128)} %bitcast.2, f32[6,16]{1,0:T(8,128)} %bitcast.3, bf16[640]{0:T(1024)(128)(2,1)} %gain_hbm.1, bf16[2,640]{1,0:T(2,128)(2,1)} %res_hbm.1, bf16[2,640]{1,0:T(2,128)(2,1)} %q_hbm.1, bf16[2,128]{1,0:T(2,128)(2,1)} %k_hbm.1, ...), custom_call_target="tpu_custom_call" | custom-call | flops 400000000 | bytes 14000000 | tf_op jit(solution)/shard_map/pallas_call | solution.py:324
  27.0 1.3 %copy.17 = bf16[2,640]{1,0:T(2,128)(2,1)} copy(bf16[2,640]{1,0:T(2,128)(2,1)} %shard_map.145) | data formatting | bytes 5120

commit v3 on v2

--- a/solution.py
+++ b/solution.py
@@ -82,12 +82,10 @@
         return lax.rem(f + k, n_kv)
 
     barrier = pltpu.get_barrier_semaphore()
-    for d in range(n_req - 1, -1, -1):
-        for k in range(n_kv):
-            if d or k:
-                pl.semaphore_signal(
-                    barrier, inc=1, device_id=(req_peer(d), kv_peer(k)), device_id_type=MESH
-                )
+    for d in range(n_req - 1, 0, -1):
+        pl.semaphore_signal(barrier, inc=1, device_id=(req_peer(d), f), device_id_type=MESH)
+    for k in range(1, n_kv):
+        pl.semaphore_signal(barrier, inc=1, device_id=(r, kv_peer(k)), device_id_type=MESH)
 
     places = (
         (q_hbm, 0, q_width),
@@ -136,7 +134,7 @@
 
     for c in small:
         c.wait()
-    pl.semaphore_wait(barrier, n_req * n_kv - 1)
+    pl.semaphore_wait(barrier, n_req + n_kv - 2)
 
     def to_req(stage, d, src, dst):
         return pltpu.make_async_remote_copy(
@@ -175,7 +173,7 @@
     inv_root = 1.0 / math.sqrt(hd)
     served = [order_ref[r * per_dev + i] for i in range(per_dev)]
     positions = lax.broadcasted_iota(jnp.int32, (1, longest), 1)
-    residual = []
+    residual, k_rows, v_rows = [], [], []
     for i in range(per_dev):
         t = served[i]
         src = t // per_dev
@@ -183,26 +181,32 @@
         which = lax.broadcasted_iota(jnp.int32, pair.shape, 0) == t - src * per_dev
         row = jnp.sum(jnp.where(which, pair, 0.0), axis=0, keepdims=True)
         residual.append(row[:, q_width + 2 * hd :])
-        k_row = row[:, q_width : q_width + hd]
-        v_row = row[:, q_width + hd : q_width + 2 * hd]
+        k_rows.append(row[:, q_width : q_width + hd])
+        v_rows.append(row[:, q_width + hd : q_width + 2 * hd])
         for h in range(heads):
             qmat[i, h : h + 1, :] = row[:, h * hd : (h + 1) * hd]
-        q = qmat[i]
-        scores = (
-            lax.dot_general(
-                q.astype(BF16), keys[i], (((1,), (1,)), ((), ())), preferred_element_type=F32
-            )
-            * inv_root
+    ques = [qmat[i] for i in range(per_dev)]
+    raw = [
+        lax.dot_general(
+            ques[i].astype(BF16), keys[i], (((1,), (1,)), ((), ())), preferred_element_type=F32
         )
-        scores = jnp.where(positions < len_ref[t], scores, -1e30)
-        own = jnp.sum(q * k_row, axis=1, keepdims=True) * inv_root
+        for i in range(per_dev)
+    ]
+    weights, own_weights, totals = [], [], []
+    for i in range(per_dev):
+        scores = jnp.where(positions < len_ref[served[i]], raw[i] * inv_root, -1e30)
+        own = jnp.sum(ques[i] * k_rows[i], axis=1, keepdims=True) * inv_root
         highest = jnp.maximum(jnp.max(scores, axis=1, keepdims=True), own)
-        weights = jnp.exp(scores - highest)
+        w = jnp.exp(scores - highest)
         own_weight = jnp.exp(own - highest)
-        totals = jnp.sum(weights, axis=1, keepdims=True) + own_weight
-        numerator = jnp.dot(weights.astype(BF16), values[i], preferred_element_type=F32)
-        numerator = numerator + own_weight.astype(BF16).astype(F32) * v_row
-        attended = numerator / totals
+        totals.append(jnp.sum(w, axis=1, keepdims=True) + own_weight)
+        weights.append(w.astype(BF16))
+        own_weights.append(own_weight.astype(BF16).astype(F32))
+    numerators = [
+        jnp.dot(weights[i], values[i], preferred_element_type=F32) for i in range(per_dev)
+    ]
+    for i in range(per_dev):
+        attended = (numerators[i] + own_weights[i] * v_rows[i]) / totals[i]
         for h in range(heads):
             att[i : i + 1, h * hd : (h + 1) * hd] = attended[h : h + 1, :]
 

time: 28.4 us -> 27.6 us (0.972)
  Pallas kernels: 26.9 us -> 26.1 us
    pallas_call x1, Pallas kernels: 26.9 us -> 26.1 us  [per_device(): pl.pallas_call(functools.partial(layer_kernel, n_req, n_kv), out_shape=ja...]
where the time goes in v3:
time: 27.6 us; the launch traced here: 27.4 us
  Pallas kernels  26.1 us (95%)
  local copies, waits for them, and re-layouts  1.26 us (5%)
    pallas_call x1, Pallas kernels, per_device(): pl.pallas_call(functools.partial(layer_kernel, n_req, n_kv), out_shape=ja...  26.1 us
    unnamed x1, local copies, waits for them, and re-layouts  1.26 us

profile of v3, /device:TPU:0, one launch (start us, length us, event | category | flops | bytes accessed | tf_op | source)
XLA Modules:
  0.0 27.4 jit_solution(13525120135441624846)
XLA Ops:
  0.0 26.1 %shard_map.145 = bf16[2,640]{1,0:T(2,128)(2,1)} custom-call(s32[16]{0:T(128)} %len_hbm.1, s32[16]{0:T(128)} %order_hbm.1, s32[6,16]{1,0:T(8,128)} %bitcast.2, f32[6,16]{1,0:T(8,128)} %bitcast.3, bf16[640]{0:T(1024)(128)(2,1)} %gain_hbm.1, bf16[2,640]{1,0:T(2,128)(2,1)} %res_hbm.1, bf16[2,640]{1,0:T(2,128)(2,1)} %q_hbm.1, bf16[2,128]{1,0:T(2,128)(2,1)} %k_hbm.1, ...), custom_call_target="tpu_custom_call" | custom-call | flops 400000000 | bytes 14000000 | tf_op jit(solution)/shard_map/pallas_call | solution.py:328
  26.1 1.3 %copy.17 = bf16[2,640]{1,0:T(2,128)(2,1)} copy(bf16[2,640]{1,0:T(2,128)(2,1)} %shard_map.145) | data formatting | bytes 5120
